TPU v7x, 32 devices: a whole 2x2x4 slice. The times are simulated.
32 devices in a mesh: ka: 16 (over z, y, core), pa: 2 (over x).
Axes of the slice: x: 2, y: 2, z: 4, core: 2. Of those that a mesh axis runs over, the one named last changes fastest.
Arguments:
- previous: float32 [128, 256, 256], P('ka', None, 'pa'), may hold values from -6 to 6
- current: float32 [128, 256, 256], P('ka', None, 'pa'), may hold values from -6 to 6
- energies: float32 [128, 256, 256], P('ka', None, 'pa'), may hold values from -0.5 to 0.5
- valence: float32 [128, 256, 256], P('ka'), may hold values from -0.375 to 0.375
- conduction: float32 [128, 256, 256], P('ka', None, 'pa'), may hold values from -0.375 to 0.375
- kernel: float32 [128, 256, 256], P(None, 'ka', 'pa'), may hold values from 0.05 to 0.35
Outputs:
- next_one: float32 [128, 256, 256], P('ka', None, 'pa')
- next_two: float32 [128, 256, 256], P('ka', None, 'pa')
All inputs are finite; a program needn't handle non-finite values.
Results may differ from a plain program's by a relative error of at most 0.000096.
Values sent between devices are 32-bit elements; how exact they have to be, the bound alone decides.
A program may use at most 64 MiB of HBM per device.

v0:
```python
import math

import jax
import jax.numpy as jnp
from jax import lax
from jax.sharding import PartitionSpec as P

KY = 16


def phase_tables(total):
    points = jnp.arange(total)
    wide = total // KY
    coarse = points // KY
    finer = points % KY
    turns = (coarse[:, None] * coarse[None, :] % wide).astype(jnp.float32) / wide
    turns = turns + (finer[:, None] * finer[None, :] % KY).astype(jnp.float32) / KY
    angles = 2.0 * math.pi * turns
    return (jnp.cos(angles), jnp.sin(angles))


def screen_owned(flattened, kernel, cosine_table, sine_table):
    highest = lax.Precision.HIGHEST
    total = kernel.shape[0]
    even = jnp.dot(cosine_table, flattened, precision=highest)
    odd = jnp.dot(sine_table, flattened, precision=highest)
    weights = kernel.reshape(total, kernel.shape[1] * kernel.shape[2])
    return (
        jnp.dot(cosine_table, weights * even, precision=highest)
        + jnp.dot(sine_table, weights * odd, precision=highest)
    ) / total


def kernel_product(field, valence, conduction, kernel, cosine_table, sine_table):
    highest = lax.Precision.HIGHEST
    total = kernel.shape[0]
    inner = jnp.einsum("kvc,kcn->kvn", field, conduction, precision=highest)
    pair_blocks = jnp.einsum("kvm,kvn->kmn", valence, inner, precision=highest)
    owned = lax.all_to_all(pair_blocks, "ka", split_axis=1, concat_axis=0, tiled=True)
    flattened = owned.reshape(total, owned.shape[1] * owned.shape[2])
    screened = screen_owned(flattened, kernel, cosine_table, sine_table).reshape(owned.shape)
    returned = lax.all_to_all(screened, "ka", split_axis=0, concat_axis=1, tiled=True)
    partial_rows = jnp.einsum("kmn,kcn->kmc", returned, conduction, precision=highest)
    return jnp.einsum("kvm,kmc->kvc", valence, partial_rows, precision=highest)


def on_device(previous, current, energies, valence, conduction, kernel):
    cosine_table, sine_table = phase_tables(kernel.shape[0])
    whole_current = lax.all_gather(current, "pa", axis=2, tiled=True)
    folded_term = kernel_product(
        whole_current, valence, conduction, kernel, cosine_table, sine_table
    )
    summed = lax.psum_scatter(folded_term, "pa", scatter_dimension=2, tiled=True)
    next_one = 2.0 * (energies * current + summed) - previous
    whole_next = lax.all_gather(next_one, "pa", axis=2, tiled=True)
    second_term = kernel_product(whole_next, valence, conduction, kernel, cosine_table, sine_table)
    second_sum = lax.psum_scatter(second_term, "pa", scatter_dimension=2, tiled=True)
    next_two = 2.0 * (energies * next_one + second_sum) - current
    return (next_one, next_two)


def solution(mesh):
    placed = (
        P("ka", None, "pa"),
        P("ka", None, "pa"),
        P("ka", None, "pa"),
        P("ka", None, None),
        P("ka", None, "pa"),
        P(None, "ka", "pa"),
    )
    return jax.shard_map(
        on_device,
        mesh=mesh,
        in_specs=placed,
        out_specs=(P("ka", None, "pa"), P("ka", None, "pa")),
        check_vma=False,
    )
```

profile of v0, /device:TPU:28, one launch (start us, length us, event | category | flops | bytes accessed | tf_op | source)
XLA Modules:
  0.0 319.2 jit_solution(2831742215432943179)
XLA Ops:
  7.9 35.7 %all-gather.3.cloned.1.call-done = f32[8,256,256]{2,1,0:T(8,128)} async-done(((f32[8,256,128]{2,1,0:T(8,128)}), f32[8,256,256]{2,1,0:T(8,128)}) %all-gather.3.cloned.1.call-update) | async-done | bytes 2097168 | tf_op jit(solution)/shard_map/all_gather | solution.py:49
  43.6 4.2 %fusion.88 = f32[8,256,128]{1,2,0:T(8,128)S(1)} fusion(f32[8,256,256]{2,1,0:T(8,128)} %all-gather.3.cloned.1.call-done, f32[8,256,128]{2,1,0:T(8,128)} %param.10), kind=kOutput, calls=%fused_computation.107 | convolution fusion | flops 805306368 | bytes 4194304 | tf_op jit(solution)/shard_map/kvc,kcn->kvn/dot_general | solution.py:37
  50.1 2.6 copy.47
  52.8 6.0 %all-to-all-start = ((f32[8,256,128]{2,0,1:T(8,128)}), f32[8,256,128]{2,0,1:T(8,128)}, u32[]{:S(2)}, u32[]{:S(2)}) async-start(f32[8,256,128]{2,0,1:T(8,128)} %copy.47), calls=%async_computation | async-start | bytes 2097152 | tf_op jit(solution)/shard_map/all_to_all | solution.py:39
  58.8 23.8 %all-to-all-done = f32[8,256,128]{2,0,1:T(8,128)} async-done(((f32[8,256,128]{2,0,1:T(8,128)}), f32[8,256,128]{2,0,1:T(8,128)}, u32[]{:S(2)}, u32[]{:S(2)}) %all-to-all-start) | async-done | bytes 1048608 | tf_op jit(solution)/shard_map/all_to_all | solution.py:39
  82.7 2.8 convolution_multiply_fusion.2
  85.5 2.8 convolution_multiply_fusion.3
  91.2 29.8 %all_to_all.66 = f32[128,16,128]{2,1,0:T(8,128)S(1)} all-to-all(f32[128,16,128]{2,1,0:T(8,128)S(1)} %bitcast.68), channel_id=1, replica_groups=mesh['ka'=16,'pa'=2] {'ka'}, dimensions={0} | all-to-all | bytes 2097152 | tf_op jit(solution)/shard_map/all_to_all | solution.py:42
  123.0 3.5 %convolution_bitcast_fusion.1 = f32[8,256,256]{1,2,0:T(8,128)} fusion(f32[8,256,256]{1,2,0:T(8,128)S(1)} %fusion.89, f32[8,256,256]{2,1,0:T(8,128)S(1)} %copy-done), kind=kOutput, calls=%fused_computation.9 | convolution fusion | flops 1610612736 | bytes 6291456 | tf_op jit(solution)/shard_map/kvm,kmc->kvc/dot_general | solution.py:44
  126.5 2.5 copy.45
  129.0 2.5 copy.44
  131.6 2.6 copy.52
  134.1 24.3 %reduce-scatter.3.cloned.1.call-done = f32[8,256,128]{1,2,0:T(8,128)} async-done(((f32[8,256,256]{1,2,0:T(8,128)}), f32[8,256,128]{1,2,0:T(8,128)}) %reduce-scatter.3.cloned.1.call-update) | async-done | bytes 1048592 | tf_op jit(solution)/shard_map/reduce_scatter | solution.py:53
  158.4 3.4 %multiply_subtract_fusion.1 = f32[8,256,128]{1,2,0:T(8,128)} fusion(f32[8,256,128]{1,2,0:T(8,128)} %copy.52, f32[8,256,128]{1,2,0:T(8,128)} %reduce-scatter.3.cloned.1.call-done, f32[8,256,128]{1,2,0:T(8,128)} %copy.44, f32[8,256,128]{1,2,0:T(8,128)} %copy.45), kind=kLoop, calls=%fused_computation.15 | loop fusion | flops 1048576 | bytes 5242880 | tf_op jit(solution)/shard_map/sub | solution.py:54
  161.9 33.2 %all-gather.5.cloned.1.call-done = f32[8,256,256]{1,2,0:T(8,128)} async-done(((f32[8,256,128]{1,2,0:T(8,128)}), f32[8,256,256]{1,2,0:T(8,128)}) %all-gather.5.cloned.1.call-update) | async-done | bytes 2097168 | tf_op jit(solution)/shard_map/all_gather | solution.py:55
  195.1 3.8 %fusion.90 = f32[8,256,128]{1,2,0:T(8,128)S(1)} fusion(f32[8,256,256]{1,2,0:T(8,128)} %all-gather.5.cloned.1.call-done, f32[8,256,128]{2,1,0:T(8,128)} %param.10), kind=kOutput, calls=%fused_computation.109 | convolution fusion | flops 805306368 | bytes 4194304 | tf_op jit(solution)/shard_map/kvc,kcn->kvn/dot_general | solution.py:37
  199.0 2.4 convolution_bitcast_fusion.2
  201.3 2.5 copy.56
  203.9 29.8 %all_to_all.67 = f32[8,256,128]{2,0,1:T(8,128)S(1)} all-to-all(f32[8,256,128]{2,0,1:T(8,128)} %copy.56), channel_id=1, replica_groups=mesh['ka'=16,'pa'=2] {'ka'}, dimensions={1} | all-to-all | bytes 2097152 | tf_op jit(solution)/shard_map/all_to_all | solution.py:39
  239.8 29.8 %all_to_all.68 = f32[128,16,128]{2,1,0:T(8,128)S(1)} all-to-all(f32[128,16,128]{2,1,0:T(8,128)S(1)} %bitcast.70), channel_id=1, replica_groups=mesh['ka'=16,'pa'=2] {'ka'}, dimensions={0} | all-to-all | bytes 2097152 | tf_op jit(solution)/shard_map/all_to_all | solution.py:42
  271.5 3.5 %convolution_bitcast_fusion = f32[8,256,256]{1,2,0:T(8,128)} fusion(f32[8,256,256]{1,2,0:T(8,128)S(1)} %fusion.91, f32[8,256,256]{2,1,0:T(8,128)S(1)} %copy-done), kind=kOutput, calls=%fused_computation.8 | convolution fusion | flops 1610612736 | bytes 6291456 | tf_op jit(solution)/shard_map/kvm,kmc->kvc/dot_general | solution.py:44
  277.5 29.5 %reduce-scatter.5.cloned.1.call-done = f32[8,256,128]{1,2,0:T(8,128)} async-done(((f32[8,256,256]{1,2,0:T(8,128)}), f32[8,256,128]{1,2,0:T(8,128)}) %reduce-scatter.5.cloned.1.call-update) | async-done | bytes 1048592 | tf_op jit(solution)/shard_map/reduce_scatter | solution.py:57
  307.0 3.1 multiply_subtract_fusion
  310.1 2.5 copy.63
  (33 shorter events, 18.6 us)
Async XLA Ops:
  7.2 40.6 %copy-start = (f32[8,256,256]{2,1,0:T(8,128)S(1)}, f32[8,256,256]{2,1,0:T(8,128)}, u32[]{:S(2)}) copy-start(f32[8,256,256]{2,1,0:T(8,128)} %param.9) | copy-start | bytes 6291460
  7.2 36.4 %all-gather.3.cloned.1.call-start = ((), (), s32[]{:S(2)}) async-start(), calls=%async_computation.6 | async-start | bytes 3145728 | tf_op jit(solution)/shard_map/all_gather | solution.py:49
  50.1 32.5 %copy-start.2 = (f32[128,16,128]{2,1,0:T(8,128)S(1)}, f32[128,16,128]{2,1,0:T(8,128)}, u32[]{:S(2)}) copy-start(f32[128,16,128]{2,1,0:T(8,128)} %param.11) | copy-start | bytes 3145732
  52.8 29.9 %all-to-all-start = ((f32[8,256,128]{2,0,1:T(8,128)}), f32[8,256,128]{2,0,1:T(8,128)}, u32[]{:S(2)}, u32[]{:S(2)}) async-start(f32[8,256,128]{2,0,1:T(8,128)} %copy.47), calls=%async_computation | async-start | bytes 2097152 | tf_op jit(solution)/shard_map/all_to_all | solution.py:39
  58.8 99.6 %reduce-scatter.3.cloned.1.call-start = ((), (), s32[]{:S(2)}) async-start(), calls=%async_computation.7 | async-start | bytes 3145728 | tf_op jit(solution)/shard_map/reduce_scatter | solution.py:53
  91.2 29.9 %copy-start.3 = (f32[8,256,128]{2,1,0:T(8,128)S(1)}, f32[8,256,128]{2,1,0:T(8,128)}, u32[]{:S(2)}) copy-start(f32[8,256,128]{2,1,0:T(8,128)} %param.10) | copy-start | bytes 3145732
  126.4 68.7 %all-gather.5.cloned.1.call-start = ((), (), s32[]{:S(2)}) async-start(), calls=%async_computation.8 | async-start | bytes 3145728 | tf_op jit(solution)/shard_map/all_gather | solution.py:55
  161.8 145.2 %reduce-scatter.5.cloned.1.call-start = ((), (), s32[]{:S(2)}) async-start(), calls=%async_computation.9 | async-start | bytes 3145728 | tf_op jit(solution)/shard_map/reduce_scatter | solution.py:57
  239.8 29.9 %copy-start.4 = (f32[8,256,128]{2,1,0:T(8,128)S(1)}, f32[8,256,128]{2,1,0:T(8,128)}, u32[]{:S(2)}) copy-start(f32[8,256,128]{2,1,0:T(8,128)} %param.10) | copy-start | bytes 3145732
  275.0 1.2 copy-start.1
Sparse Core Ops, SparseCore 0:
  9.5 34.0 all-gather.2
  126.5 31.8 reduce-scatter.2
  162.0 33.1 all-gather.4
  275.1 31.8 reduce-scatter.4
where the time goes:
time: 322 us; the launch traced here: 319 us
  waiting for transfers between devices  147 us (46%)
  blocking collectives  89.4 us (28%)
  matrix products  37.5 us (12%)
  local copies, waits for them, and re-layouts  18.4 us (6%)
  between operations  13.9 us (4%)
  other arithmetic  6.53 us (2%)
  starting transfers between devices  6.18 us (2%)
    all_to_all x2, blocking collectives, kernel_product(): lax.all_to_all(screened, 'ka', split_axis=0, concat_axis=1, tiled=True)  59.5 us
    all_gather x1, waiting for transfers between devices, on_device(): whole_current = lax.all_gather(current, 'pa', axis=2, tiled=True)  35.7 us
    all_gather x1, waiting for transfers between devices, on_device(): whole_next = lax.all_gather(next_one, 'pa', axis=2, tiled=True)  33.2 us
    all_to_all x1, blocking collectives, kernel_product(): lax.all_to_all(pair_blocks, 'ka', split_axis=1, concat_axis=0, tiled=True)  29.8 us
    reduce_scatter x1, waiting for transfers between devices, on_device(): lax.psum_scatter(second_term, 'pa', scatter_dimension=2, tiled=True)  29.5 us
    reduce_scatter x1, waiting for transfers between devices, on_device(): lax.psum_scatter(folded_term, 'pa', scatter_dimension=2, tiled=True)  24.3 us
    all_to_all x1, waiting for transfers between devices, kernel_product(): lax.all_to_all(pair_blocks, 'ka', split_axis=1, concat_axis=0, tiled=True)  23.8 us
    unnamed x17, local copies, waits for them, and re-layouts  13.1 us
  transfers between devices with their start and end apart: 5, of which 5 were waited for; matrix products, arithmetic and copies ran while one was open for 3% of the time, Pallas kernels for 0%

commit v1 on v0

--- a/solution.py
+++ b/solution.py
@@ -1,11 +1,359 @@
+import functools
 import math
 
 import jax
 import jax.numpy as jnp
 from jax import lax
+from jax.experimental import pallas as pl
+from jax.experimental.pallas import tpu as pltpu
 from jax.sharding import PartitionSpec as P
 
 KY = 16
+MESH = pl.DeviceIdType.MESH
+LAG_NEXT = 1
+LAG_PAIRS = 2
+
+
+def plus(a, b, sign=1.0):
+    re = a[0] + b[0] if sign > 0 else a[0] - b[0]
+    if b[1] is None:
+        return (re, a[1])
+    if a[1] is None:
+        return (re, b[1] if sign > 0 else -b[1])
+    return (re, a[1] + b[1] if sign > 0 else a[1] - b[1])
+
+
+def conj(a):
+    return a if a[1] is None else (a[0], -a[1])
+
+
+def turn(a, step, size, sign):
+    eighth = 8 * step // size if 8 * step % size == 0 else None
+    if eighth == 0:
+        return a
+    if eighth == 2:
+        re = None if a[1] is None else (-a[1] if sign > 0 else a[1])
+        im = a[0] if sign > 0 else -a[0]
+        return (jnp.zeros_like(im) if re is None else re, im)
+    c = math.cos(2.0 * math.pi * step / size)
+    s = sign * math.sin(2.0 * math.pi * step / size)
+    if a[1] is None:
+        return (c * a[0], s * a[0])
+    if eighth == 1:
+        return (c * (a[0] - sign * a[1]), c * (a[1] + sign * a[0]))
+    if eighth == 3:
+        return (c * (a[0] + sign * a[1]), c * (a[1] - sign * a[0]))
+    return (c * a[0] - s * a[1], c * a[1] + s * a[0])
+
+
+def complex_transform(x, sign):
+    size = len(x)
+    if size == 1:
+        return x
+    even = complex_transform(x[0::2], sign)
+    odd = complex_transform(x[1::2], sign)
+    odd = [turn(o, j, size, sign) for j, o in enumerate(odd)]
+    first = [plus(e, o) for e, o in zip(even, odd)]
+    return first + [plus(e, o, -1.0) for e, o in zip(even, odd)]
+
+
+def real_forward(x):
+    size = len(x)
+    if size == 1:
+        return [(x[0], None)]
+    even, odd = real_forward(x[0::2]), real_forward(x[1::2])
+    if size == 2:
+        return [plus(even[0], odd[0]), plus(even[0], odd[0], -1.0)]
+    out = [None] * (size // 2 + 1)
+    for j in range(size // 4):
+        t = turn(odd[j], j, size, -1)
+        out[j] = plus(even[j], t)
+        out[size // 2 - j] = conj(plus(even[j], t, -1.0))
+    out[size // 4] = (even[size // 4][0], -odd[size // 4][0])
+    return out
+
+
+def real_backward(spectrum):
+    size = 2 * (len(spectrum) - 1)
+    if size == 2:
+        a, b = spectrum[0][0], spectrum[1][0]
+        return [a + b, a - b]
+    even, odd = [], []
+    for j in range(size // 4):
+        mirrored = conj(spectrum[size // 2 - j])
+        even.append(plus(spectrum[j], mirrored))
+        odd.append(turn(plus(spectrum[j], mirrored, -1.0), j, size, 1))
+    middle = spectrum[size // 4]
+    even.append((2.0 * middle[0], None))
+    odd.append((-2.0 * middle[1], None))
+    out = [None] * size
+    out[0::2] = real_backward(even)
+    out[1::2] = real_backward(odd)
+    return out
+
+
+def screen_in_place(ref, weights):
+    total, rows = ref.shape[0], ref.shape[1]
+    wide = total // KY
+    half = KY // 2
+    scale = 0.5 / total
+    assert rows % 8 == 0
+
+    def fine_forward(i, carry):
+        base, at = (i % wide) * KY, pl.ds(pl.multiple_of((i // wide) * 8, 8), 8)
+        out = real_forward([ref[base + j, at, :] for j in range(KY)])
+        for j in range(half + 1):
+            ref[base + j, at, :] = out[j][0]
+            if 0 < j < half:
+                ref[base + KY - j, at, :] = out[j][1]
+        return carry
+
+    def fine_backward(i, carry):
+        base, at = (i % wide) * KY, pl.ds(pl.multiple_of((i // wide) * 8, 8), 8)
+        values = [ref[base + j, at, :] for j in range(KY)]
+        spectrum = [(values[0], None)]
+        spectrum += [(values[j], values[KY - j]) for j in range(1, half)]
+        spectrum += [(values[half], None)]
+        for j, value in enumerate(real_backward(spectrum)):
+            ref[base + j, at, :] = value
+        return carry
+
+    def weight(q, finer, mirror, at):
+        a = weights[q * KY + finer, at, :]
+        b = weights[((wide - q) % wide) * KY + mirror, at, :]
+        return (a + b) * scale
+
+    def coarse_real(i, carry):
+        at = pl.ds(pl.multiple_of(i * 8, 8), 8)
+        for finer in (0, half):
+            out = real_forward([ref[j * KY + finer, at, :] for j in range(wide)])
+            scaled = []
+            for q, (re, im) in enumerate(out):
+                w = weight(q, finer, finer, at)
+                scaled.append((re * w, None if im is None else im * w))
+            for j, value in enumerate(real_backward(scaled)):
+                ref[j * KY + finer, at, :] = value
+        return carry
+
+    def coarse_complex(i, carry):
+        finer = 1 + i % (half - 1)
+        mirror = KY - finer
+        at = pl.ds(pl.multiple_of((i // (half - 1)) * 8, 8), 8)
+        x = [(ref[j * KY + finer, at, :], ref[j * KY + mirror, at, :]) for j in range(wide)]
+        scaled = []
+        for q, (re, im) in enumerate(complex_transform(x, -1)):
+            w = weight(q, finer, mirror, at)
+            scaled.append((re * w, im * w))
+        for j, (re, im) in enumerate(complex_transform(scaled, 1)):
+            ref[j * KY + finer, at, :] = re
+            ref[j * KY + mirror, at, :] = im
+        return carry
+
+    blocks = rows // 8
+    lax.fori_loop(0, blocks * wide, fine_forward, 0)
+    lax.fori_loop(0, blocks, coarse_real, 0)
+    lax.fori_loop(0, blocks * (half - 1), coarse_complex, 0)
+    lax.fori_loop(0, blocks * wide, fine_backward, 0)
+
+
+def split(a):
+    high = a.astype(jnp.bfloat16)
+    return high, (a - high.astype(jnp.float32)).astype(jnp.bfloat16)
+
+
+def product(a, b, left, right):
+    dot = functools.partial(
+        lax.dot_general,
+        dimension_numbers=(((left,), (right,)), ((), ())),
+        preferred_element_type=jnp.float32,
+    )
+    (ah, al), (bh, bl) = split(a), split(b)
+    return dot(ah, bh) + (dot(ah, bl) + dot(al, bh))
+
+
+def fused_kernel(
+    ka, previous, current, energies, valence, conduction, weights, next_one, next_two,
+    other_x, pairs, owned, returned, sent_sum, other_sum, own_sum,
+    x_send, x_recv, pair_send, pair_recv, back_send, back_recv, sum_send, sum_recv,
+):
+    me, mine = lax.axis_index("ka"), lax.axis_index("pa")
+    other = 1 - mine
+    count, _, width = current.shape
+    rows = weights.shape[1]
+    own_c = pl.ds(pl.multiple_of(mine * width, width), width)
+    other_c = pl.ds(pl.multiple_of(other * width, width), width)
+    own_rows = pl.ds(pl.multiple_of(me * rows, rows), rows)
+
+    barrier = pltpu.get_barrier_semaphore()
+
+    def greet(j, carry):
+        pl.semaphore_signal(
+            barrier, inc=1, device_id={"ka": lax.rem(me + j, ka)}, device_id_type=MESH
+        )
+        return carry
+
+    lax.fori_loop(1, ka, greet, 0)
+    pl.semaphore_signal(barrier, inc=1, device_id={"pa": other}, device_id_type=MESH)
+    pl.semaphore_wait(barrier, ka)
+
+    def x_copy(turn_, k):
+        source = (current, next_one)[turn_]
+        return pltpu.make_async_remote_copy(
+            src_ref=source.at[k], dst_ref=other_x.at[turn_, k],
+            send_sem=x_send.at[turn_, k], recv_sem=x_recv.at[turn_, k],
+            device_id={"pa": other}, device_id_type=MESH,
+        )
+
+    def sum_copy(turn_, k):
+        return pltpu.make_async_remote_copy(
+            src_ref=sent_sum.at[turn_, k], dst_ref=other_sum.at[turn_, k],
+            send_sem=sum_send.at[turn_, k], recv_sem=sum_recv.at[turn_, k],
+            device_id={"pa": other}, device_id_type=MESH,
+        )
+
+    def both_halves(k):
+        return jnp.concatenate([conduction[k, own_c, :], conduction[k, other_c, :]], axis=0)
+
+    def pair_step(turn_, k):
+        source = (current, next_one)[turn_]
+        x_copy(turn_, k).wait_recv()
+        x = jnp.concatenate([source[k], other_x[turn_, k]], axis=1)
+        inner = product(x, both_halves(k), 1, 0)
+        pairs[turn_, k] = product(valence[k], inner, 0, 0)
+
+        def send(j, carry):
+            peer = lax.rem(me + j, ka)
+            pltpu.make_async_remote_copy(
+                src_ref=pairs.at[turn_, k, pl.ds(pl.multiple_of(peer * rows, rows), rows)],
+                dst_ref=owned.at[turn_, me * count + k],
+                send_sem=pair_send.at[turn_], recv_sem=pair_recv.at[turn_],
+                device_id={"ka": peer}, device_id_type=MESH,
+            ).start()
+            return carry
+
+        lax.fori_loop(1, ka, send, 0)
+        owned[turn_, me * count + k] = pairs[turn_, k, own_rows, :]
+
+    def wait_bytes(ref, sem):
+        pltpu.make_async_copy(ref, ref, sem).wait()
+
+    def screen(turn_):
+        wait_bytes(owned.at[turn_, pl.ds(0, (ka - 1) * count)], pair_recv.at[turn_])
+        screen_in_place(owned.at[turn_], weights)
+
+        def send(i, carry):
+            k, j = i // (ka - 1), 1 + i % (ka - 1)
+            peer = lax.rem(me + j, ka)
+            pltpu.make_async_remote_copy(
+                src_ref=owned.at[turn_, peer * count + k],
+                dst_ref=returned.at[turn_, k, own_rows],
+                send_sem=back_send.at[turn_], recv_sem=back_recv.at[turn_, k],
+                device_id={"ka": peer}, device_id_type=MESH,
+            ).start()
+            return carry
+
+        lax.fori_loop(0, count * (ka - 1), send, 0)
+
+        def keep(k, carry):
+            returned[turn_, k, own_rows, :] = owned[turn_, me * count + k]
+            return carry
+
+        lax.fori_loop(0, count, keep, 0)
+
+    def sum_step(turn_, k):
+        wait_bytes(returned.at[turn_, k, pl.ds(0, (ka - 1) * rows)], back_recv.at[turn_, k])
+        partial_rows = product(returned[turn_, k], both_halves(k), 1, 1)
+        term = product(valence[k], partial_rows, 1, 0)
+        sent_sum[turn_, k] = term[:, width:]
+        sum_copy(turn_, k).start()
+        own_sum[k] = term[:, :width]
+
+    def next_step(turn_, k):
+        sum_copy(turn_, k).wait_recv()
+        summed = own_sum[k] + other_sum[turn_, k]
+        if turn_ == 0:
+            next_one[k] = 2.0 * (energies[k] * current[k] + summed) - previous[k]
+            x_copy(1, k).start()
+        else:
+            next_two[k] = 2.0 * (energies[k] * next_one[k] + summed) - current[k]
+
+    def start_x(k, carry):
+        x_copy(0, k).start()
+        return carry
+
+    lax.fori_loop(0, count, start_x, 0)
+
+    def first_pairs(k, carry):
+        pair_step(0, k)
+        return carry
+
+    lax.fori_loop(0, count, first_pairs, 0)
+    screen(0)
+
+    def middle(t, carry):
+        @pl.when(t < count)
+        def _():
+            sum_step(0, t)
+
+        @pl.when(jnp.logical_and(t >= LAG_NEXT, t < count + LAG_NEXT))
+        def _():
+            next_step(0, t - LAG_NEXT)
+
+        @pl.when(t >= LAG_PAIRS)
+        def _():
+            pair_step(1, t - LAG_PAIRS)
+
+        return carry
+
+    lax.fori_loop(0, count + LAG_PAIRS, middle, 0)
+    screen(1)
+
+    def last(t, carry):
+        @pl.when(t < count)
+        def _():
+            sum_step(1, t)
+
+        @pl.when(t >= LAG_NEXT)
+        def _():
+            next_step(1, t - LAG_NEXT)
+
+        return carry
+
+    lax.fori_loop(0, count + LAG_NEXT, last, 0)
+
+    for turn_ in (0, 1):
+        def sent(k, carry):
+            x_copy(turn_, k).wait_send()
+            sum_copy(turn_, k).wait_send()
+            return carry
+
+        lax.fori_loop(0, count, sent, 0)
+        everything = owned.at[turn_, pl.ds(0, (ka - 1) * count)]
+        wait_bytes(everything, pair_send.at[turn_])
+        wait_bytes(everything, back_send.at[turn_])
+
+
+def fused(ka, previous, current, energies, valence, conduction, kernel):
+    block, owned = current.shape, kernel.shape
+    whole = pl.BlockSpec(memory_space=pltpu.VMEM)
+    points = (block[0], valence.shape[2], kernel.shape[2])
+    twice = lambda shape: pltpu.VMEM((2,) + shape, jnp.float32)
+    dma = pltpu.SemaphoreType.DMA
+    return pl.pallas_call(
+        functools.partial(fused_kernel, ka),
+        out_shape=(jax.ShapeDtypeStruct(block, jnp.float32),) * 2,
+        in_specs=[whole] * 6,
+        out_specs=(whole, whole),
+        scratch_shapes=[
+            twice(block), twice(points), twice(owned), twice(points),
+            twice(block), twice(block), pltpu.VMEM(block, jnp.float32),
+            dma((2, block[0])), dma((2, block[0])), dma((2,)), dma((2,)),
+            dma((2,)), dma((2, block[0])), dma((2, block[0])), dma((2, block[0])),
+        ],
+        compiler_params=pltpu.CompilerParams(
+            collective_id=0, has_side_effects=True, vmem_limit_bytes=52 * 2**20
+        ),
+    )(previous, current, energies, valence, conduction, kernel)
 
 
 def phase_tables(total):
@@ -44,7 +392,21 @@
     return jnp.einsum("kvm,kmc->kvc", valence, partial_rows, precision=highest)
 
 
-def on_device(previous, current, energies, valence, conduction, kernel):
+def fits(ka, pa, current, conduction, kernel):
+    wide = kernel.shape[0] // KY
+    return (
+        pa == 2
+        and current.shape[2] == kernel.shape[2]
+        and current.shape[2] % 128 == 0
+        and kernel.shape[1] % 8 == 0
+        and wide >= 2
+        and wide & (wide - 1) == 0
+    )
+
+
+def on_device(ka, pa, previous, current, energies, valence, conduction, kernel):
+    if fits(ka, pa, current, conduction, kernel):
+        return fused(ka, previous, current, energies, valence, conduction, kernel)
     cosine_table, sine_table = phase_tables(kernel.shape[0])
     whole_current = lax.all_gather(current, "pa", axis=2, tiled=True)
     folded_term = kernel_product(
@@ -69,7 +431,7 @@
         P(None, "ka", "pa"),
     )
     return jax.shard_map(
-        on_device,
+        functools.partial(on_device, mesh.shape["ka"], mesh.shape["pa"]),
         mesh=mesh,
         in_specs=placed,
         out_specs=(P("ka", None, "pa"), P("ka", None, "pa")),

time: 322 us -> 141 us (0.44)
  waiting for transfers between devices: 147 us -> 0 us
  Pallas kernels: 0 us -> 137 us
  blocking collectives: 89.4 us -> 0 us
  matrix products: 37.5 us -> 0 us
  local copies, waits for them, and re-layouts: 18.4 us -> 2.57 us
  between operations: 13.9 us -> 0.65 us
  other arithmetic: 6.53 us -> 0 us
  starting transfers between devices: 6.18 us -> 0 us
    pallas_call x0 -> x1, Pallas kernels: none -> 137 us  [fused(): pl.pallas_call(functools.partial(fused_kernel, ka), out_shape=(jax.ShapeD...]
    all_to_all x3 -> x0, blocking collectives: 89.4 us -> none  [the longest x2 59.5 us: kernel_product(): lax.all_to_all(screened, 'ka', split_axis=0, concat_axis=1, tiled=True)]
    all_gather x2 -> x0, waiting for transfers between devices: 68.9 us -> none  [the longest x1 35.7 us: on_device(): whole_current = lax.all_gather(current, 'pa', axis=2, tiled=True)]
    reduce_scatter x2 -> x0, waiting for transfers between devices: 53.8 us -> none  [the longest x1 29.5 us: on_device(): lax.psum_scatter(second_term, 'pa', scatter_dimension=2, tiled=True)]
    dot_general x16 -> x0, matrix products: 37.5 us -> none  [the longest x2 8.02 us: kernel_product(): inner = jnp.einsum('kvc,kcn->kvn', field, conduction, precision=highest)]
    all_to_all x1 -> x0, waiting for transfers between devices: 23.8 us -> none  [kernel_product(): lax.all_to_all(pair_blocks, 'ka', split_axis=1, concat_axis=0, tiled=True)]
    unnamed x17 -> x4, local copies, waits for them, and re-layouts: 13.1 us -> 2.57 us
    sub x2 -> x0, other arithmetic: 6.53 us -> none  [the longest x1 3.41 us: on_device(): next_one = 2.0 * (energies * current + summed) - previous]
  transfers between devices with their start and end apart: 5 -> 0, of which waited for: 5 -> 0; matrix products, arithmetic and copies ran while one was open for 3% -> 0% of each run, Pallas kernels for 0% -> 0%
where the time goes in v1:
time: 141 us; the launch traced here: 140 us
  Pallas kernels  137 us (97%)
  local copies, waits for them, and re-layouts  2.57 us (2%)
    pallas_call x1, Pallas kernels, fused(): pl.pallas_call(functools.partial(fused_kernel, ka), out_shape=(jax.ShapeD...  137 us

profile of v1, /device:TPU:28, one launch (start us, length us, event | category | flops | bytes accessed | tf_op | source)
XLA Modules:
  0.0 140.2 jit_solution(12693747861042693279)
XLA Ops:
  0.6 137.0 %shard_map.77 = (f32[8,256,128]{2,1,0:T(8,128)S(1)}, f32[8,256,128]{2,1,0:T(8,128)}) custom-call(f32[8,256,128]{2,1,0:T(8,128)} %previous.1, f32[8,256,128]{2,1,0:T(8,128)} %current.1, f32[8,256,128]{2,1,0:T(8,128)} %energies.1, f32[8,256,256]{2,1,0:T(8,128)} %valence.1, f32[8,256,128]{2,1,0:T(8,128)} %conduction.1, f32[128,16,128]{2,1,0:T(8,128)} %weights.1), custom_call_target="tpu_custom_call" | custom-call | tf_op jit(solution)/shard_map/pallas_call | solution.py:342
  137.6 0.0 copy-start
  137.6 1.0 copy.10
  138.6 0.6 copy-done
  139.2 1.0 copy.11
Async XLA Ops:
  137.6 1.6 %copy-start = (f32[8,256,128]{2,1,0:T(8,128)S(1)}, f32[8,256,128]{2,1,0:T(8,128)}, u32[]{:S(2)}) copy-start(f32[8,256,128]{2,1,0:T(8,128)} %get-tuple-element.5) | copy-start | bytes 3145732

commit v2 on v1

--- a/solution.py
+++ b/solution.py
@@ -10,8 +10,9 @@
 
 KY = 16
 MESH = pl.DeviceIdType.MESH
-LAG_NEXT = 1
-LAG_PAIRS = 2
+LAG_NEXT = 2
+LAG_PAIRS = 4
+AHEAD = 3
 
 
 def plus(a, b, sign=1.0):
@@ -217,6 +218,10 @@
     def pair_step(turn_, k):
         source = (current, next_one)[turn_]
         x_copy(turn_, k).wait_recv()
+        if turn_ == 0:
+            @pl.when(k + AHEAD < count)
+            def _():
+                x_copy(0, k + AHEAD).start()
         x = jnp.concatenate([source[k], other_x[turn_, k]], axis=1)
         inner = product(x, both_halves(k), 1, 0)
         pairs[turn_, k] = product(valence[k], inner, 0, 0)
@@ -237,12 +242,8 @@
     def wait_bytes(ref, sem):
         pltpu.make_async_copy(ref, ref, sem).wait()
 
-    def screen(turn_):
-        wait_bytes(owned.at[turn_, pl.ds(0, (ka - 1) * count)], pair_recv.at[turn_])
-        screen_in_place(owned.at[turn_], weights)
-
-        def send(i, carry):
-            k, j = i // (ka - 1), 1 + i % (ka - 1)
+    def send_back(turn_, k):
+        def send(j, carry):
             peer = lax.rem(me + j, ka)
             pltpu.make_async_remote_copy(
                 src_ref=owned.at[turn_, peer * count + k],
@@ -252,7 +253,14 @@
             ).start()
             return carry
 
-        lax.fori_loop(0, count * (ka - 1), send, 0)
+        lax.fori_loop(1, ka, send, 0)
+
+    def screen(turn_):
+        wait_bytes(owned.at[turn_, pl.ds(0, (ka - 1) * count)], pair_recv.at[turn_])
+        screen_in_place(owned.at[turn_], weights)
+
+        for k in range(min(AHEAD, count)):
+            send_back(turn_, k)
 
         def keep(k, carry):
             returned[turn_, k, own_rows, :] = owned[turn_, me * count + k]
@@ -262,6 +270,11 @@
 
     def sum_step(turn_, k):
         wait_bytes(returned.at[turn_, k, pl.ds(0, (ka - 1) * rows)], back_recv.at[turn_, k])
+
+        @pl.when(k + AHEAD < count)
+        def _():
+            send_back(turn_, k + AHEAD)
+
         partial_rows = product(returned[turn_, k], both_halves(k), 1, 1)
         term = product(valence[k], partial_rows, 1, 0)
         sent_sum[turn_, k] = term[:, width:]
@@ -281,7 +294,7 @@
         x_copy(0, k).start()
         return carry
 
-    lax.fori_loop(0, count, start_x, 0)
+    lax.fori_loop(0, min(AHEAD, count), start_x, 0)
 
     def first_pairs(k, carry):
         pair_step(0, k)

time: 141 us -> 140 us (level)
  no operation moved by 1% of the time
where the time goes in v2:
time: 140 us
  Pallas kernels  136 us (97%)
  local copies, waits for them, and re-layouts  2.57 us (2%)
    pallas_call x1, Pallas kernels, fused(): pl.pallas_call(functools.partial(fused_kernel, ka), out_shape=(jax.ShapeD...  136 us

profile of v2, /device:TPU:28, one launch (start us, length us, event | category | flops | bytes accessed | tf_op | source)
XLA Modules:
  0.0 139.5 jit_solution(7522230006162059578)
XLA Ops:
  0.6 136.3 %shard_map.77 = (f32[8,256,128]{2,1,0:T(8,128)S(1)}, f32[8,256,128]{2,1,0:T(8,128)}) custom-call(f32[8,256,128]{2,1,0:T(8,128)} %previous.1, f32[8,256,128]{2,1,0:T(8,128)} %current.1, f32[8,256,128]{2,1,0:T(8,128)} %energies.1, f32[8,256,256]{2,1,0:T(8,128)} %valence.1, f32[8,256,128]{2,1,0:T(8,128)} %conduction.1, f32[128,16,128]{2,1,0:T(8,128)} %weights.1), custom_call_target="tpu_custom_call" | custom-call | tf_op jit(solution)/shard_map/pallas_call | solution.py:355
  136.9 0.0 copy-start
  136.9 1.0 copy.10
  137.9 0.6 copy-done
  138.5 1.0 copy.11
Async XLA Ops:
  136.9 1.6 %copy-start = (f32[8,256,128]{2,1,0:T(8,128)S(1)}, f32[8,256,128]{2,1,0:T(8,128)}, u32[]{:S(2)}) copy-start(f32[8,256,128]{2,1,0:T(8,128)} %get-tuple-element.5) | copy-start | bytes 3145732

commit v3 on v2

--- a/solution.py
+++ b/solution.py
@@ -13,6 +13,7 @@
 LAG_NEXT = 2
 LAG_PAIRS = 4
 AHEAD = 3
+GROUP = 2
 
 
 def plus(a, b, sign=1.0):
@@ -163,18 +164,19 @@
 
 
 def product(a, b, left, right):
-    dot = functools.partial(
-        lax.dot_general,
+    (ah, al), (bh, bl) = a, b
+    return lax.dot_general(
+        jnp.concatenate([ah, ah, al], axis=left),
+        jnp.concatenate([bh, bl, bh], axis=right),
         dimension_numbers=(((left,), (right,)), ((), ())),
         preferred_element_type=jnp.float32,
     )
-    (ah, al), (bh, bl) = split(a), split(b)
-    return dot(ah, bh) + (dot(ah, bl) + dot(al, bh))
 
 
 def fused_kernel(
     ka, previous, current, energies, valence, conduction, weights, next_one, next_two,
     other_x, pairs, owned, returned, sent_sum, other_sum, own_sum,
+    turned_parts, valence_parts, conduction_parts,
     x_send, x_recv, pair_send, pair_recv, back_send, back_recv, sum_send, sum_recv,
 ):
     me, mine = lax.axis_index("ka"), lax.axis_index("pa")
@@ -212,8 +214,15 @@
             device_id={"pa": other}, device_id_type=MESH,
         )
 
-    def both_halves(k):
-        return jnp.concatenate([conduction[k, own_c, :], conduction[k, other_c, :]], axis=0)
+    def prepare(k, carry):
+        rows_of = jnp.concatenate([conduction[k, own_c, :], conduction[k, other_c, :]], axis=0)
+        conduction_parts[0, k], conduction_parts[1, k] = split(rows_of)
+        valence_parts[0, k], valence_parts[1, k] = split(valence[k])
+        turned_parts[0, k], turned_parts[1, k] = split(valence[k].T)
+        return carry
+
+    def parts(ref, k):
+        return ref[0, k], ref[1, k]
 
     def pair_step(turn_, k):
         source = (current, next_one)[turn_]
@@ -223,44 +232,44 @@
             def _():
                 x_copy(0, k + AHEAD).start()
         x = jnp.concatenate([source[k], other_x[turn_, k]], axis=1)
-        inner = product(x, both_halves(k), 1, 0)
-        pairs[turn_, k] = product(valence[k], inner, 0, 0)
-
-        def send(j, carry):
+        inner = product(split(x), parts(conduction_parts, k), 1, 0)
+        pairs[turn_, k] = product(parts(turned_parts, k), split(inner), 1, 0)
+
+        owned[turn_, me * count + k] = pairs[turn_, k, own_rows, :]
+
+        @pl.when(k % GROUP == GROUP - 1)
+        def _():
+            start = k - (GROUP - 1)
+            for j in range(1, ka):
+                peer = lax.rem(me + j, ka)
+                mark = pl.ds(pl.multiple_of(peer * rows, rows), rows)
+                pltpu.make_async_remote_copy(
+                    src_ref=pairs.at[turn_, pl.ds(start, GROUP), mark],
+                    dst_ref=owned.at[turn_, pl.ds(me * count + start, GROUP)],
+                    send_sem=pair_send.at[turn_], recv_sem=pair_recv.at[turn_],
+                    device_id={"ka": peer}, device_id_type=MESH,
+                ).start()
+
+    def wait_bytes(ref, sem):
+        pltpu.make_async_copy(ref, ref, sem).wait()
+
+    def send_back(turn_, g):
+        for j in range(1, ka):
             peer = lax.rem(me + j, ka)
             pltpu.make_async_remote_copy(
-                src_ref=pairs.at[turn_, k, pl.ds(pl.multiple_of(peer * rows, rows), rows)],
-                dst_ref=owned.at[turn_, me * count + k],
-                send_sem=pair_send.at[turn_], recv_sem=pair_recv.at[turn_],
+                src_ref=owned.at[turn_, pl.ds(peer * count + g * GROUP, GROUP)],
+                dst_ref=returned.at[turn_, pl.ds(g * GROUP, GROUP), own_rows],
+                send_sem=back_send.at[turn_], recv_sem=back_recv.at[turn_, g],
                 device_id={"ka": peer}, device_id_type=MESH,
             ).start()
-            return carry
-
-        lax.fori_loop(1, ka, send, 0)
-        owned[turn_, me * count + k] = pairs[turn_, k, own_rows, :]
-
-    def wait_bytes(ref, sem):
-        pltpu.make_async_copy(ref, ref, sem).wait()
-
-    def send_back(turn_, k):
-        def send(j, carry):
-            peer = lax.rem(me + j, ka)
-            pltpu.make_async_remote_copy(
-                src_ref=owned.at[turn_, peer * count + k],
-                dst_ref=returned.at[turn_, k, own_rows],
-                send_sem=back_send.at[turn_], recv_sem=back_recv.at[turn_, k],
-                device_id={"ka": peer}, device_id_type=MESH,
-            ).start()
-            return carry
-
-        lax.fori_loop(1, ka, send, 0)
 
     def screen(turn_):
         wait_bytes(owned.at[turn_, pl.ds(0, (ka - 1) * count)], pair_recv.at[turn_])
         screen_in_place(owned.at[turn_], weights)
 
-        for k in range(min(AHEAD, count)):
-            send_back(turn_, k)
+        send_back(turn_, 0)
+        if count > GROUP:
+            send_back(turn_, 1)
 
         def keep(k, carry):
             returned[turn_, k, own_rows, :] = owned[turn_, me * count + k]
@@ -269,14 +278,18 @@
         lax.fori_loop(0, count, keep, 0)
 
     def sum_step(turn_, k):
-        wait_bytes(returned.at[turn_, k, pl.ds(0, (ka - 1) * rows)], back_recv.at[turn_, k])
-
-        @pl.when(k + AHEAD < count)
-        def _():
-            send_back(turn_, k + AHEAD)
-
-        partial_rows = product(returned[turn_, k], both_halves(k), 1, 1)
-        term = product(valence[k], partial_rows, 1, 0)
+        @pl.when(k % GROUP == 0)
+        def _():
+            g = k // GROUP
+            group = pl.ds(k, GROUP)
+            wait_bytes(returned.at[turn_, group, pl.ds(0, (ka - 1) * rows)], back_recv.at[turn_, g])
+
+            @pl.when(g + 2 < count // GROUP)
+            def _():
+                send_back(turn_, g + 2)
+
+        partial_rows = product(split(returned[turn_, k]), parts(conduction_parts, k), 1, 1)
+        term = product(parts(valence_parts, k), split(partial_rows), 1, 0)
         sent_sum[turn_, k] = term[:, width:]
         sum_copy(turn_, k).start()
         own_sum[k] = term[:, :width]
@@ -295,6 +308,7 @@
         return carry
 
     lax.fori_loop(0, min(AHEAD, count), start_x, 0)
+    lax.fori_loop(0, count, prepare, 0)
 
     def first_pairs(k, carry):
         pair_step(0, k)
@@ -351,6 +365,7 @@
     whole = pl.BlockSpec(memory_space=pltpu.VMEM)
     points = (block[0], valence.shape[2], kernel.shape[2])
     twice = lambda shape: pltpu.VMEM((2,) + shape, jnp.float32)
+    halves = lambda *shape: pltpu.VMEM((2,) + shape, jnp.bfloat16)
     dma = pltpu.SemaphoreType.DMA
     return pl.pallas_call(
         functools.partial(fused_kernel, ka),
@@ -360,6 +375,8 @@
         scratch_shapes=[
             twice(block), twice(points), twice(owned), twice(points),
             twice(block), twice(block), pltpu.VMEM(block, jnp.float32),
+            halves(points[0], points[1], valence.shape[1]), halves(*valence.shape),
+            halves(*conduction.shape),
             dma((2, block[0])), dma((2, block[0])), dma((2,)), dma((2,)),
             dma((2,)), dma((2, block[0])), dma((2, block[0])), dma((2, block[0])),
         ],
@@ -412,6 +429,7 @@
         and current.shape[2] == kernel.shape[2]
         and current.shape[2] % 128 == 0
         and kernel.shape[1] % 8 == 0
+        and current.shape[0] % GROUP == 0
         and wide >= 2
         and wide & (wide - 1) == 0
     )

time: 140 us -> 152 us (1.086)
  Pallas kernels: 136 us -> 149 us
    pallas_call x1, Pallas kernels: 136 us -> 149 us  [fused(): pl.pallas_call(functools.partial(fused_kernel, ka), out_shape=(jax.ShapeD...]
where the time goes in v3:
time: 152 us
  Pallas kernels  149 us (98%)
  local copies, waits for them, and re-layouts  2.57 us (2%)
    pallas_call x1, Pallas kernels, fused(): pl.pallas_call(functools.partial(fused_kernel, ka), out_shape=(jax.ShapeD...  149 us

profile of v3, /device:TPU:28, one launch (start us, length us, event | category | flops | bytes accessed | tf_op | source)
XLA Modules:
  0.0 152.2 jit_solution(7266760872502094115)
XLA Ops:
  0.6 149.0 %shard_map.77 = (f32[8,256,128]{2,1,0:T(8,128)S(1)}, f32[8,256,128]{2,1,0:T(8,128)}) custom-call(f32[8,256,128]{2,1,0:T(8,128)} %previous.1, f32[8,256,128]{2,1,0:T(8,128)} %current.1, f32[8,256,128]{2,1,0:T(8,128)} %energies.1, f32[8,256,256]{2,1,0:T(8,128)} %valence.1, f32[8,256,128]{2,1,0:T(8,128)} %conduction.1, f32[128,16,128]{2,1,0:T(8,128)} %weights.1), custom_call_target="tpu_custom_call" | custom-call | tf_op jit(solution)/shard_map/pallas_call | solution.py:370
  149.6 0.0 copy-start
  149.7 1.0 copy.10
  150.6 0.6 copy-done
  151.2 1.0 copy.11
Async XLA Ops:
  149.6 1.6 %copy-start = (f32[8,256,128]{2,1,0:T(8,128)S(1)}, f32[8,256,128]{2,1,0:T(8,128)}, u32[]{:S(2)}) copy-start(f32[8,256,128]{2,1,0:T(8,128)} %get-tuple-element.5) | copy-start | bytes 3145732

commit v4 on v3

--- a/solution.py
+++ b/solution.py
@@ -13,7 +13,7 @@
 LAG_NEXT = 2
 LAG_PAIRS = 4
 AHEAD = 3
-GROUP = 2
+GROUP = 1
 
 
 def plus(a, b, sign=1.0):
@@ -174,10 +174,11 @@
 
 
 def fused_kernel(
-    ka, previous, current, energies, valence, conduction, weights, next_one, next_two,
+    ka, previous_in, current_in, energies_in, valence_in, conduction_in, weights_in,
+    next_one, next_two, previous, current, energies, valence, conduction, weights,
     other_x, pairs, owned, returned, sent_sum, other_sum, own_sum,
     turned_parts, valence_parts, conduction_parts,
-    x_send, x_recv, pair_send, pair_recv, back_send, back_recv, sum_send, sum_recv,
+    load_sem, x_send, x_recv, pair_send, pair_recv, back_send, back_recv, sum_send, sum_recv,
 ):
     me, mine = lax.axis_index("ka"), lax.axis_index("pa")
     other = 1 - mine
@@ -187,6 +188,15 @@
     other_c = pl.ds(pl.multiple_of(other * width, width), width)
     own_rows = pl.ds(pl.multiple_of(me * rows, rows), rows)
 
+    def load(i):
+        pairs_of = (
+            (conduction_in, conduction), (valence_in, valence), (current_in, current),
+            (weights_in, weights), (energies_in, energies), (previous_in, previous),
+        )
+        return pltpu.make_async_copy(pairs_of[i][0], pairs_of[i][1], load_sem.at[i])
+
+    for i in range(6):
+        load(i).start()
     barrier = pltpu.get_barrier_semaphore()
 
     def greet(j, carry):
@@ -200,7 +210,7 @@
     pl.semaphore_wait(barrier, ka)
 
     def x_copy(turn_, k):
-        source = (current, next_one)[turn_]
+        source = (current_in, next_one)[turn_]
         return pltpu.make_async_remote_copy(
             src_ref=source.at[k], dst_ref=other_x.at[turn_, k],
             send_sem=x_send.at[turn_, k], recv_sem=x_recv.at[turn_, k],
@@ -267,9 +277,8 @@
         wait_bytes(owned.at[turn_, pl.ds(0, (ka - 1) * count)], pair_recv.at[turn_])
         screen_in_place(owned.at[turn_], weights)
 
-        send_back(turn_, 0)
-        if count > GROUP:
-            send_back(turn_, 1)
+        for g in range(min(AHEAD, count // GROUP)):
+            send_back(turn_, g)
 
         def keep(k, carry):
             returned[turn_, k, own_rows, :] = owned[turn_, me * count + k]
@@ -284,9 +293,9 @@
             group = pl.ds(k, GROUP)
             wait_bytes(returned.at[turn_, group, pl.ds(0, (ka - 1) * rows)], back_recv.at[turn_, g])
 
-            @pl.when(g + 2 < count // GROUP)
+            @pl.when(g + AHEAD < count // GROUP)
             def _():
-                send_back(turn_, g + 2)
+                send_back(turn_, g + AHEAD)
 
         partial_rows = product(split(returned[turn_, k]), parts(conduction_parts, k), 1, 1)
         term = product(parts(valence_parts, k), split(partial_rows), 1, 0)
@@ -308,13 +317,18 @@
         return carry
 
     lax.fori_loop(0, min(AHEAD, count), start_x, 0)
+    load(0).wait()
+    load(1).wait()
     lax.fori_loop(0, count, prepare, 0)
+    load(2).wait()
 
     def first_pairs(k, carry):
         pair_step(0, k)
         return carry
 
     lax.fori_loop(0, count, first_pairs, 0)
+    for i in (3, 4, 5):
+        load(i).wait()
     screen(0)
 
     def middle(t, carry):
@@ -361,6 +375,7 @@
 
 
 def fused(ka, previous, current, energies, valence, conduction, kernel):
+    arrays = (previous, current, energies, valence, conduction, kernel)
     block, owned = current.shape, kernel.shape
     whole = pl.BlockSpec(memory_space=pltpu.VMEM)
     points = (block[0], valence.shape[2], kernel.shape[2])
@@ -370,20 +385,21 @@
     return pl.pallas_call(
         functools.partial(fused_kernel, ka),
         out_shape=(jax.ShapeDtypeStruct(block, jnp.float32),) * 2,
-        in_specs=[whole] * 6,
+        in_specs=[pl.BlockSpec(memory_space=pl.ANY)] * 6,
         out_specs=(whole, whole),
         scratch_shapes=[
+            *(pltpu.VMEM(a.shape, jnp.float32) for a in arrays),
             twice(block), twice(points), twice(owned), twice(points),
             twice(block), twice(block), pltpu.VMEM(block, jnp.float32),
             halves(points[0], points[1], valence.shape[1]), halves(*valence.shape),
             halves(*conduction.shape),
-            dma((2, block[0])), dma((2, block[0])), dma((2,)), dma((2,)),
+            dma((6,)), dma((2, block[0])), dma((2, block[0])), dma((2,)), dma((2,)),
             dma((2,)), dma((2, block[0])), dma((2, block[0])), dma((2, block[0])),
         ],
         compiler_params=pltpu.CompilerParams(
             collective_id=0, has_side_effects=True, vmem_limit_bytes=52 * 2**20
         ),
-    )(previous, current, energies, valence, conduction, kernel)
+    )(*arrays)
 
 
 def phase_tables(total):

time: 152 us -> 136 us (0.89)
  Pallas kernels: 149 us -> 132 us
    pallas_call x1, Pallas kernels: 149 us -> 132 us  [fused(): pl.pallas_call(functools.partial(fused_kernel, ka), out_shape=(jax.ShapeD...]
where the time goes in v4:
time: 136 us; the launch traced here: 135 us
  Pallas kernels  132 us (97%)
  local copies, waits for them, and re-layouts  2.57 us (2%)
    pallas_call x1, Pallas kernels, fused(): pl.pallas_call(functools.partial(fused_kernel, ka), out_shape=(jax.ShapeD...  132 us

profile of v4, /device:TPU:28, one launch (start us, length us, event | category | flops | bytes accessed | tf_op | source)
XLA Modules:
  0.0 135.3 jit_solution(8626119446976540749)
XLA Ops:
  0.6 132.1 %shard_map.77 = (f32[8,256,128]{2,1,0:T(8,128)S(1)}, f32[8,256,128]{2,1,0:T(8,128)}) custom-call(f32[8,256,128]{2,1,0:T(8,128)} %previous_in.1, f32[8,256,128]{2,1,0:T(8,128)} %current_in.1, f32[8,256,128]{2,1,0:T(8,128)} %energies_in.1, f32[8,256,256]{2,1,0:T(8,128)} %valence_in.1, f32[8,256,128]{2,1,0:T(8,128)} %conduction_in.1, f32[128,16,128]{2,1,0:T(8,128)} %weights_in.1), custom_call_target="tpu_custom_call" | custom-call | tf_op jit(solution)/shard_map/pallas_call | solution.py:385
  132.7 0.0 copy-start
  132.7 1.0 copy.10
  133.7 0.6 copy-done
  134.3 1.0 copy.11
Async XLA Ops:
  132.7 1.6 %copy-start = (f32[8,256,128]{2,1,0:T(8,128)S(1)}, f32[8,256,128]{2,1,0:T(8,128)}, u32[]{:S(2)}) copy-start(f32[8,256,128]{2,1,0:T(8,128)} %get-tuple-element.5) | copy-start | bytes 3145732
